TPU v7x, 32 devices: a whole 2x2x4 slice. The times are simulated.
32 devices in a mesh: dp: 32 (over z, y, x, core).
Axes of the slice: x: 2, y: 2, z: 4, core: 2. Of those that a mesh axis runs over, the one named last changes fastest.
Arguments:
- partials: bfloat16 [32, 256, 16384], P('dp'), may hold values from -24 to 24
- master: float32 [256, 16384], P('dp'), may hold values from -3 to 3
- moment_one: float32 [256, 16384], P('dp'), may hold values from -2 to 2
- moment_two: float32 [256, 16384], P('dp'), may hold values from 0.01 to 1
Outputs:
- master_new: float32 [256, 16384], P('dp')
- moment_one_new: float32 [256, 16384], P('dp')
- moment_two_new: float32 [256, 16384], P('dp')
- reduced_grad: float32 [256, 16384], P('dp')
- weights: bfloat16 [256, 16384], replicated
All inputs are finite; a program needn't handle non-finite values. Where the computation divides by a largest or mean magnitude, that divisor is 1e-20 or more.
Results may differ from a plain program's by a relative error of at most 0.012.
Values may be sent and summed in bfloat16 or wider, within the bound.
A program may use at most 128 MiB of HBM per device.

v0:
```python
import jax
import jax.numpy as jnp
from jax import lax
from jax.sharding import PartitionSpec as P

BLOCK = 128
MBITS = 7
STEP = 20


def block_scale(amax):
    powers = jnp.asarray([2.0**k for k in range(-20, 13)], jnp.float32)
    doubled = jnp.asarray([2.0 ** (k + 1) for k in range(-20, 13)], jnp.float32)
    inverse = jnp.asarray([2.0 ** (MBITS - k - 1) for k in range(-20, 13)], jnp.float32)
    hit = amax[..., None] >= powers
    scale = jnp.max(jnp.where(hit, doubled, jnp.float32(2.0 ** (-20))), axis=-1)
    mult = jnp.min(jnp.where(hit, inverse, jnp.float32(2.0 ** (MBITS + 20))), axis=-1)
    return (scale, mult)


def per_device(partials, master, moment_one, moment_two):
    devices = lax.axis_size("dp")
    local = partials[0]
    rows = local.shape[0]
    width = local.shape[1]
    nblk = width // BLOCK
    owned = master.shape[0]
    mags = jnp.abs(local.astype(jnp.float32)).reshape(rows, nblk, BLOCK)
    shared = lax.pmax(jnp.max(mags, axis=2).astype(jnp.bfloat16), "dp").astype(jnp.float32)
    scale_all, mult = block_scale(shared)
    vals = local.astype(jnp.float32).reshape(rows, nblk, BLOCK) * mult[:, :, None]
    mant = jnp.floor(vals + 0.5).reshape(rows, width)
    total = lax.psum_scatter(mant, "dp", scatter_dimension=0, tiled=True)
    start = lax.axis_index("dp") * owned
    scale = lax.dynamic_slice_in_dim(scale_all, start, owned, 0)
    total = total.reshape(owned, nblk, BLOCK)
    factor = scale / (2.0**MBITS * devices)
    reduced_grad = (total * factor[:, :, None]).reshape(owned, width)
    moment_one_new = 0.9 * moment_one + 0.1 * reduced_grad
    moment_two_new = 0.95 * moment_two + 0.05 * reduced_grad * reduced_grad
    first = moment_one_new / (1.0 - 0.9**STEP)
    second = moment_two_new / (1.0 - 0.95**STEP)
    update = first / (jnp.sqrt(second) + 1e-08)
    master_new = master - 0.001 * (update + 0.1 * master)
    blocks = master_new.reshape(owned, nblk, BLOCK)
    wscale = jnp.max(jnp.abs(blocks), axis=2) + 1e-06
    wmant = (blocks / wscale[:, :, None]).astype(jnp.bfloat16)
    own_weights = (
        (wmant.astype(jnp.float32) * wscale[:, :, None]).reshape(owned, width).astype(jnp.bfloat16)
    )
    weights = lax.all_gather(own_weights, "dp", axis=0, tiled=True)
    return (master_new, moment_one_new, moment_two_new, reduced_grad, weights)


def solution(mesh):
    in_specs = (P("dp", None, None), P("dp", None), P("dp", None), P("dp", None))
    out_specs = (P("dp", None), P("dp", None), P("dp", None), P("dp", None), P())
    return jax.shard_map(
        per_device, mesh=mesh, in_specs=in_specs, out_specs=out_specs, check_vma=False
    )
```

profile of v0, /device:TPU:1, one launch (start us, length us, event | category | flops | bytes accessed | tf_op | source)
XLA Modules:
  0.0 457.2 jit_solution(9559224516611359040)
XLA Ops:
  7.2 0.0 all-reduce.2.cloned.1.call-start
  7.2 9.6 %fusion.3 = bf16[32,8,128,128]{3,1,2,0:T(8,128)(2,1)} fusion(bf16[1,256,16384]{2,1,0:T(8,128)(2,1)} %param.7), kind=kLoop, calls=%fused_computation.5 | loop fusion | flops 12582912 | bytes 16777216
  16.8 9.2 %copy.13 = bf16[32,8,128,128]{3,2,1,0:T(8,128)(2,1)} copy(bf16[32,8,128,128]{3,1,2,0:T(8,128)(2,1)} %fusion.3) | data formatting | bytes 16777216
  26.0 0.0 copy-start.4
  26.0 0.0 copy-start.5
  26.0 0.0 copy-start.6
  26.0 6.4 %reduce_max.27 = bf16[256,128]{1,0:T(8,128)(2,1)} reduce(bf16[256,128,128]{2,1,0:T(8,128)(2,1)} %bitcast.30, bf16[]{:T(256)} %constant.66), dimensions={2}, to_apply=%region_0.0 | reduce | flops 4161536 | bytes 8454146 | tf_op jit(solution)/shard_map/reduce_max | solution.py:29
  32.3 0.0 all-reduce.2.cloned.1.call-update
  32.4 0.0 reduce-scatter.2.cloned.1.call-start
  32.4 121.6 %all-reduce.2.cloned.1.call-done = bf16[256,128]{1,0:T(8,128)(2,1)} async-done(((bf16[256,128]{1,0:T(8,128)(2,1)}), bf16[256,128]{1,0:T(8,128)(2,1)}) %all-reduce.2.cloned.1.call-update) | async-done | bytes 65552 | tf_op jit(solution)/shard_map/pmax | solution.py:29
  154.0 0.8 convert_element_type.38
  154.9 0.0 copy-done.4
  154.9 0.0 copy-done.5
  154.9 0.0 copy-done.6
  154.9 0.8 fusion.5
  155.8 4.6 %mul.67 = f32[256,128,128]{2,1,0:T(8,128)S(1)} broadcast(f32[256,128]{1,0:T(8,128)S(1)} %get-tuple-element.6), dimensions={0,1} | broadcast | bytes 16908288 | tf_op jit(solution)/shard_map/mul | solution.py:31
  160.4 17.3 %fusion.2 = f32[256,16384]{1,0:T(8,128)} fusion(bf16[1,256,16384]{2,1,0:T(8,128)(2,1)} %param.7, f32[32,8,128,128]{3,2,1,0:T(8,128)S(1)} %bitcast.29), kind=kLoop, calls=%fused_computation.4 | loop fusion | flops 16777216 | bytes 41943040 | tf_op jit(solution)/shard_map/floor | solution.py:32
  177.7 0.0 copy-start.1
  177.7 0.0 copy-start.2
  177.7 0.0 copy-start.3
  177.7 0.0 reduce-scatter.2.cloned.1.call-update
  177.7 0.0 all-gather.2.cloned.1.call-start
  177.8 0.1 copy.12
  177.9 182.2 %reduce-scatter.2.cloned.1.call-done = f32[8,16384]{1,0:T(8,128)} async-done(((f32[256,16384]{1,0:T(8,128)}), f32[8,16384]{1,0:T(8,128)}) %reduce-scatter.2.cloned.1.call-update) | async-done | bytes 524304 | tf_op jit(solution)/shard_map/reduce_scatter | solution.py:33
  360.1 0.0 copy-done.1
  360.1 0.0 copy-done.2
  360.1 0.0 copy-done.3
  360.1 2.6 bitcast_reduce_fusion
  362.7 0.0 copy-start
  362.7 0.9 fusion.8
  363.6 0.0 all-gather.2.cloned.1.call-update
  363.7 79.3 %all-gather.2.cloned.1.call-done = bf16[256,16384]{1,0:T(8,128)(2,1)} async-done(((bf16[8,16384]{1,0:T(8,128)(2,1)}), bf16[256,16384]{1,0:T(8,128)(2,1)}) %all-gather.2.cloned.1.call-update) | async-done | bytes 8388624 | tf_op jit(solution)/shard_map/all_gather | solution.py:51
  443.0 7.7 %copy.18 = bf16[256,16384]{1,0:T(8,128)(2,1)} copy(bf16[256,16384]{1,0:T(8,128)(2,1)} %all-gather.2.cloned.1.call-done) | data formatting | bytes 16777216
  450.6 0.0 copy-done
  (2 shorter events, 0.0 us)
Async XLA Ops:
  7.2 146.9 %all-reduce.2.cloned.1.call-start = ((), (), s32[]{:S(2)}) async-start(), calls=%async_computation.1 | async-start | bytes 131072 | tf_op jit(solution)/shard_map/pmax | solution.py:29
  26.0 128.9 %copy-start.4 = (f32[33]{0:T(128)S(1)}, f32[33]{0:T(128)}, u32[]{:S(2)}) copy-start(f32[33]{0:T(128)} %constant.51.clone) | copy-start | bytes 400
  26.0 128.9 %copy-start.5 = (f32[33]{0:T(128)S(1)}, f32[33]{0:T(128)}, u32[]{:S(2)}) copy-start(f32[33]{0:T(128)} %constant.50.clone) | copy-start | bytes 400
  26.0 129.0 %copy-start.6 = (f32[33]{0:T(128)S(1)}, f32[33]{0:T(128)}, u32[]{:S(2)}) copy-start(f32[33]{0:T(128)} %constant.49.clone) | copy-start | bytes 400
  32.4 327.7 %reduce-scatter.2.cloned.1.call-start = ((), (), s32[]{:S(2)}) async-start(), calls=%async_computation.2 | async-start | bytes 17301504 | tf_op jit(solution)/shard_map/reduce_scatter | solution.py:33
  177.7 182.4 %copy-start.1 = (f32[8,16384]{1,0:T(8,128)S(1)}, f32[8,16384]{1,0:T(8,128)}, u32[]{:S(2)}) copy-start(f32[8,16384]{1,0:T(8,128)} %param.8) | copy-start | bytes 1572868
  177.7 182.4 %copy-start.2 = (f32[8,16384]{1,0:T(8,128)S(1)}, f32[8,16384]{1,0:T(8,128)}, u32[]{:S(2)}) copy-start(f32[8,16384]{1,0:T(8,128)} %param.9) | copy-start | bytes 1572868
  177.7 182.4 %copy-start.3 = (f32[8,16384]{1,0:T(8,128)S(1)}, f32[8,16384]{1,0:T(8,128)}, u32[]{:S(2)}) copy-start(f32[8,16384]{1,0:T(8,128)} %param.10) | copy-start | bytes 1572868
  177.7 265.3 %all-gather.2.cloned.1.call-start = ((), (), s32[]{:S(2)}) async-start(), calls=%async_computation.3 | async-start | bytes 8650752 | tf_op jit(solution)/shard_map/all_gather | solution.py:51
  362.7 87.9 %copy-start = (f32[8,16384]{1,0:T(8,128)}, f32[8,16384]{1,0:T(8,128)S(1)}, u32[]{:S(2)}) copy-start(f32[8,16384]{1,0:T(8,128)S(1)} %get-tuple-element.17) | copy-start | bytes 1572868
Sparse Core Ops, SparseCore 0:
  32.5 121.5 all-reduce.1
  177.8 182.2 reduce-scatter.1
  363.8 79.1 all-gather.1
where the time goes:
time: 458 us; the launch traced here: 457 us
  waiting for transfers between devices  383 us (84%)
  other arithmetic  38.4 us (8%)
  local copies, waits for them, and re-layouts  21.6 us (5%)
  between operations  13.8 us (3%)
    reduce_scatter x1, waiting for transfers between devices, per_device(): total = lax.psum_scatter(mant, 'dp', scatter_dimension=0, tiled=True)  182 us
    pmax x1, waiting for transfers between devices, per_device(): lax.pmax(jnp.max(mags, axis=2).astype(jnp.bfloat16), 'dp')  122 us
    all_gather x1, waiting for transfers between devices, per_device(): weights = lax.all_gather(own_weights, 'dp', axis=0, tiled=True)  79.3 us
    floor x1, other arithmetic, per_device(): mant = jnp.floor(vals + 0.5).reshape(rows, width)  17.3 us
    unnamed x16, local copies, waits for them, and re-layouts  16.9 us
    unnamed x1, other arithmetic  9.56 us
  transfers between devices with their start and end apart: 3, of which 3 were waited for; matrix products, arithmetic and copies ran while one was open for 0% of the time, Pallas kernels for 0%

commit v1 on v0

--- a/solution.py
+++ b/solution.py
@@ -1,11 +1,498 @@
+import functools
+
 import jax
 import jax.numpy as jnp
 from jax import lax
+from jax.experimental import pallas as pl
+from jax.experimental.pallas import tpu as pltpu
 from jax.sharding import PartitionSpec as P
 
 BLOCK = 128
 MBITS = 7
 STEP = 20
+CHUNKS = 4
+F32 = jnp.float32
+BF16 = jnp.bfloat16
+
+
+def adam(grad, master, one, two):
+    one_new = 0.9 * one + 0.1 * grad
+    two_new = 0.95 * two + 0.05 * grad * grad
+    first = one_new / (1.0 - 0.9**STEP)
+    second = two_new / (1.0 - 0.95**STEP)
+    update = first / (jnp.sqrt(second) + 1e-08)
+    return master - 0.001 * (update + 0.1 * master), one_new, two_new
+
+
+def kernel(
+    n,
+    half,
+    parts,
+    master,
+    one,
+    two,
+    master_new,
+    one_new,
+    two_new,
+    grad_out,
+    weights,
+    own,
+    peer,
+    pair,
+    amax,
+    top_tx,
+    top_rx,
+    mult,
+    factor,
+    quad_rx,
+    quad,
+    duo_rx,
+    duo,
+    solo_rx,
+    decoded,
+    grad,
+    w_tx,
+    w_rows,
+    gathered,
+    load_sem,
+    peer_send,
+    peer_recv,
+    top_send,
+    top_recv,
+    quad_send,
+    quad_recv,
+    duo_send,
+    duo_recv,
+    solo_send,
+    solo_recv,
+    grad_send,
+    grad_recv,
+    row_send,
+    row_recv,
+    g_send,
+    g_recv,
+    out_sem,
+    out_send,
+    out_recv,
+):
+    me = lax.axis_index("dp")
+    core = me % 2
+    x = (me // 2) % 2
+    y = (me // 4) % 2
+    z0 = (me // 8) % 2
+    z1 = me // 16
+    chip = me // 2
+    other_core = me + 1 - 2 * core
+    over_x = me + 2 * (1 - 2 * x)
+    over_y = me + 4 * (1 - 2 * y)
+    over_xy = over_x + 4 * (1 - 2 * y)
+    over_z0 = me + 8 * (1 - 2 * z0)
+    over_z1 = me + 16 * (1 - 2 * z1)
+    over_z01 = over_z0 + 16 * (1 - 2 * z1)
+    plane = (over_x, over_y, over_xy)
+    line = (over_z0, over_z1, over_z01)
+    width = half // CHUNKS
+    nblk = width // BLOCK
+    mine = core * half
+    theirs = (1 - core) * half
+
+    def remote(src, dst, send, recv, device):
+        return pltpu.make_async_remote_copy(
+            src_ref=src,
+            dst_ref=dst,
+            send_sem=send,
+            recv_sem=recv,
+            device_id=(device,),
+            device_id_type=pl.DeviceIdType.MESH,
+        )
+
+    def at(start, size=width):
+        return pl.ds(pl.multiple_of(start, BLOCK), size)
+
+    loads = []
+    for j in range(CHUNKS):
+        c = pl.ds(j * width, width)
+        loads.append(
+            pltpu.make_async_copy(
+                parts.at[:, :, :, :, :, at(mine + j * width)],
+                own.at[:, :, :, :, :, c],
+                load_sem.at[j],
+            )
+        )
+        loads[j].start()
+
+    barrier = pltpu.get_barrier_semaphore()
+    for device in (other_core,) + plane + line:
+        pl.semaphore_signal(
+            barrier, inc=1, device_id=(device,), device_id_type=pl.DeviceIdType.MESH
+        )
+    pl.semaphore_wait(barrier, 7)
+
+    swaps = []
+    for j in range(CHUNKS):
+        c = pl.ds(j * width, width)
+        swaps.append(
+            remote(
+                parts.at[:, :, :, :, :, at(theirs + j * width)],
+                peer.at[:, :, :, :, :, c],
+                peer_send.at[j],
+                peer_recv.at[j],
+                other_core,
+            )
+        )
+        swaps[j].start()
+
+    amax[...] = jnp.zeros_like(amax)
+    lanes = lax.broadcasted_iota(jnp.int32, (BLOCK, BLOCK), 1)
+    subs = lax.broadcasted_iota(jnp.int32, (BLOCK, BLOCK), 0)
+    shift = half // BLOCK
+
+    def block_max(b, _):
+        c = at(b * BLOCK, BLOCK)
+        for h in range(2):
+            a = jnp.abs(own[h, :, :, :, :, c].reshape(BLOCK, BLOCK).astype(F32))
+            p = jnp.abs(peer[h, :, :, :, :, c].reshape(BLOCK, BLOCK).astype(F32))
+            m = jnp.max(jnp.maximum(a, p), axis=1, keepdims=True)
+            amax[...] = jnp.where(lanes == b + h * shift, m, amax[...])
+        return 0
+
+    for j in range(CHUNKS):
+        loads[j].wait()
+        swaps[j].wait_recv()
+        lax.fori_loop(j * nblk, (j + 1) * nblk, block_max, 0)
+
+    for r, group in enumerate((plane, line)):
+        top_tx[r] = amax[...].astype(BF16)
+        copies = [
+            remote(
+                top_tx.at[r], top_rx.at[r, i], top_send.at[r, i], top_recv.at[r, i], device
+            )
+            for i, device in enumerate(group)
+        ]
+        for copy in copies:
+            copy.start()
+        for i, copy in enumerate(copies):
+            copy.wait_recv()
+        best = amax[...]
+        for i in range(3):
+            best = jnp.maximum(best, top_rx[r, i].astype(F32))
+        amax[...] = best
+        for copy in copies:
+            copy.wait_send()
+
+    top = amax[...]
+    m = jnp.full((BLOCK, BLOCK), 2.0 ** (MBITS + 20), F32)
+    f = jnp.full((BLOCK, BLOCK), 2.0**-20 / (2.0**MBITS * n), F32)
+    for k in range(-20, 13):
+        hit = top >= 2.0**k
+        m = jnp.where(hit, 2.0 ** (MBITS - k - 1), m)
+        f = jnp.where(hit, 2.0 ** (k + 1) / (2.0**MBITS * n), f)
+    mult[...] = m.astype(BF16)
+    factor[...] = f
+
+    def spread(values, lane):
+        pick = jnp.where(subs == lane, 1.0, 0.0).astype(BF16)
+        return jnp.dot(values, pick, preferred_element_type=F32)
+
+    def block_pair(b, _):
+        c = at(b * BLOCK, BLOCK)
+        for h in range(2):
+            s = spread(mult[...], b + h * shift)
+            a = own[h, :, :, :, :, c].reshape(BLOCK, BLOCK).astype(F32)
+            p = peer[h, :, :, :, :, c].reshape(BLOCK, BLOCK).astype(F32)
+            t = jnp.floor(a * s + 0.5) + jnp.floor(p * s + 0.5)
+            pair[h, :, :, :, :, c] = t.astype(BF16).reshape(2, 2, 2, 16, BLOCK)
+        return 0
+
+    started = {}
+
+    def start(j, key, copies):
+        for copy in copies:
+            copy.start()
+        started[j, key] = copies
+
+    def arrived(j, key):
+        for copy in started[j, key]:
+            copy.wait_recv()
+
+    def cols(j):
+        return pl.ds(j * width, width)
+
+    def send_pair(j):
+        lax.fori_loop(j * nblk, (j + 1) * nblk, block_pair, 0)
+        c = cols(j)
+        spots = ((y, 1 - x), (1 - y, x), (1 - y, 1 - x))
+        start(
+            j,
+            "quad",
+            [
+                remote(
+                    pair.at[:, :, yy, xx, :, c],
+                    quad_rx.at[i, :, :, :, c],
+                    quad_send.at[j, i],
+                    quad_recv.at[j, i],
+                    device,
+                )
+                for i, ((yy, xx), device) in enumerate(zip(spots, plane))
+            ],
+        )
+
+    def send_quad(j):
+        arrived(j, "quad")
+
+        def body(b, _):
+            c = at(b * BLOCK, BLOCK)
+            t = pair[:, :, y, x, :, c].astype(F32)
+            for i in range(3):
+                t = t + quad_rx[i, :, :, :, c].astype(F32)
+            quad[:, :, :, c] = t
+            return 0
+
+        lax.fori_loop(j * nblk, (j + 1) * nblk, body, 0)
+        c = cols(j)
+        start(
+            j,
+            "duo",
+            [
+                remote(
+                    quad.at[:, 1 - z0, :, c],
+                    duo_rx.at[:, :, c],
+                    duo_send.at[j],
+                    duo_recv.at[j],
+                    over_z0,
+                )
+            ],
+        )
+
+    def send_duo(j):
+        arrived(j, "duo")
+        c = cols(j)
+        duo[:, :, c] = quad[:, z0, :, c] + duo_rx[:, :, c]
+        start(
+            j,
+            "solo",
+            [
+                remote(
+                    duo.at[1 - z1, :, c],
+                    solo_rx.at[:, c],
+                    solo_send.at[j],
+                    solo_recv.at[j],
+                    over_z1,
+                )
+            ],
+        )
+
+    def send_grad(j):
+        arrived(j, "solo")
+        rows = pl.ds(pl.multiple_of((chip % 8) * 16, 16), 16)
+        scales = factor[rows, :]
+
+        def body(b, _):
+            c = at(b * BLOCK, BLOCK)
+            lane = b + (chip // 8) * shift
+            near = jnp.where(lanes[:16] == lane, scales, 0.0)
+            s = jnp.sum(near, axis=1, keepdims=True)
+            t = (duo[z1, :, c] + solo_rx[:, c]) * s
+            decoded[:, :, c] = t.reshape(2, 8, BLOCK)
+            return 0
+
+        lax.fori_loop(j * nblk, (j + 1) * nblk, body, 0, unroll=4)
+        c = cols(j)
+        grad[core, :, c] = decoded[core, :, c]
+        start(
+            j,
+            "grad",
+            [
+                remote(
+                    decoded.at[1 - core, :, c],
+                    grad.at[core, :, c],
+                    grad_send.at[j],
+                    grad_recv.at[j],
+                    other_core,
+                )
+            ],
+        )
+
+    def step(j, h):
+        c = cols(j)
+        far = at(h * half + j * width)
+        g = grad[h, :, c]
+        new, m1, m2 = adam(g, master[:, far], one[:, far], two[:, far])
+        master_new[:, far] = new
+        one_new[:, far] = m1
+        two_new[:, far] = m2
+        grad_out[:, far] = g
+        blocks = []
+        for i in range(nblk):
+            v = new[:, i * BLOCK : (i + 1) * BLOCK]
+            w = jnp.max(jnp.abs(v), axis=1, keepdims=True) + 1e-06
+            blocks.append((v / w).astype(BF16).astype(F32) * w)
+        return jnp.concatenate(blocks, axis=1)
+
+    def send_rows(j):
+        arrived(j, "grad")
+        c = cols(j)
+        w_tx[:, c] = step(j, 1 - core)
+        start(
+            j,
+            "rows",
+            [
+                remote(
+                    w_tx.at[:, c],
+                    w_rows.at[core, :, c],
+                    row_send.at[j],
+                    row_recv.at[j],
+                    other_core,
+                )
+            ],
+        )
+        w_rows[core, :, c] = step(j, core)
+
+    def gather(j, key, i, spot, device):
+        ref = gathered.at[spot]
+        return remote(ref, ref, g_send.at[j, i], g_recv.at[j, i], device)
+
+    def gather_z1(j):
+        arrived(j, "rows")
+        c = cols(j)
+        gathered[z1, z0, y, x, :, c] = w_rows[:, :, c].reshape(16, width).astype(BF16)
+        start(j, "g1", [gather(j, "g1", 0, (z1, z0, y, x, slice(None), c), over_z1)])
+
+    def gather_z0(j):
+        arrived(j, "g1")
+        c = cols(j)
+        start(j, "g2", [gather(j, "g2", 1, (slice(None), z0, y, x, slice(None), c), over_z0)])
+
+    def streams(j):
+        return (
+            pl.ds(j * width, width // 2),
+            pl.ds(j * width + width // 2, width // 2),
+        )
+
+    every = slice(None)
+
+    def gather_first(j):
+        arrived(j, "g2")
+        ca, cb = streams(j)
+        start(
+            j,
+            "g3",
+            [
+                gather(j, "g3", 2, (every, every, y, x, every, ca), over_y),
+                gather(j, "g3", 3, (every, every, y, x, every, cb), over_x),
+            ],
+        )
+
+    def gather_second(j):
+        arrived(j, "g3")
+        ca, cb = streams(j)
+        start(
+            j,
+            "g4",
+            [
+                gather(j, "g4", 4, (every, every, every, x, every, ca), over_x),
+                gather(j, "g4", 5, (every, every, y, every, every, cb), over_y),
+            ],
+        )
+
+    local = {}
+
+    def hand_out(j):
+        arrived(j, "g4")
+        c = cols(j)
+        src = gathered.at[:, :, :, :, :, c]
+        dst = weights.at[:, :, :, :, :, at(mine + j * width)]
+        start(j, "out", [remote(src, dst, out_send.at[j], out_recv.at[j], other_core)])
+        local[j] = pltpu.make_async_copy(src, dst, out_sem.at[j])
+        local[j].start()
+
+    stages = (
+        send_pair,
+        send_quad,
+        send_duo,
+        send_grad,
+        send_rows,
+        gather_z1,
+        gather_z0,
+        gather_first,
+        gather_second,
+        hand_out,
+    )
+    for t in range(CHUNKS + len(stages) - 1):
+        for s in range(len(stages)):
+            if 0 <= t - s < CHUNKS:
+                stages[s](t - s)
+    for j in range(CHUNKS):
+        arrived(j, "out")
+        local[j].wait()
+        swaps[j].wait_send()
+    for copies in started.values():
+        for copy in copies:
+            copy.wait_send()
+
+
+def fused(partials, master, moment_one, moment_two):
+    n = lax.axis_size("dp")
+    rows, full = partials.shape[1:]
+    half = full // 2
+    dims = (2, 2, 2, 2, 16)
+    vmem = pl.BlockSpec(memory_space=pltpu.VMEM)
+    hbm = pl.BlockSpec(memory_space=pl.ANY)
+    state = jax.ShapeDtypeStruct(master.shape, F32)
+    dma = pltpu.SemaphoreType.DMA
+    outs = pl.pallas_call(
+        functools.partial(kernel, n, half),
+        out_shape=(state,) * 4 + (jax.ShapeDtypeStruct(dims + (full,), BF16),),
+        in_specs=[hbm, vmem, vmem, vmem],
+        out_specs=(vmem,) * 4 + (hbm,),
+        scratch_shapes=[
+            pltpu.VMEM(dims + (half,), BF16),
+            pltpu.VMEM(dims + (half,), BF16),
+            pltpu.VMEM(dims + (half,), BF16),
+            pltpu.VMEM((BLOCK, BLOCK), F32),
+            pltpu.VMEM((2, BLOCK, BLOCK), BF16),
+            pltpu.VMEM((2, 3, BLOCK, BLOCK), BF16),
+            pltpu.VMEM((BLOCK, BLOCK), BF16),
+            pltpu.VMEM((BLOCK, BLOCK), F32),
+            pltpu.VMEM((3, 2, 2, 16, half), BF16),
+            pltpu.VMEM((2, 2, 16, half), F32),
+            pltpu.VMEM((2, 16, half), F32),
+            pltpu.VMEM((2, 16, half), F32),
+            pltpu.VMEM((16, half), F32),
+            pltpu.VMEM((2, 8, half), F32),
+            pltpu.VMEM((2, 8, half), F32),
+            pltpu.VMEM((8, half), F32),
+            pltpu.VMEM((2, 8, half), F32),
+            pltpu.VMEM(dims + (half,), BF16),
+            dma((CHUNKS,)),
+            dma((CHUNKS,)),
+            dma((CHUNKS,)),
+            dma((2, 3)),
+            dma((2, 3)),
+            dma((CHUNKS, 3)),
+            dma((CHUNKS, 3)),
+            dma((CHUNKS,)),
+            dma((CHUNKS,)),
+            dma((CHUNKS,)),
+            dma((CHUNKS,)),
+            dma((CHUNKS,)),
+            dma((CHUNKS,)),
+            dma((CHUNKS,)),
+            dma((CHUNKS,)),
+            dma((CHUNKS, 6)),
+            dma((CHUNKS, 6)),
+            dma((CHUNKS,)),
+            dma((CHUNKS,)),
+            dma((CHUNKS,)),
+        ],
+        compiler_params=pltpu.CompilerParams(
+            collective_id=0, has_side_effects=True, vmem_limit_bytes=56 * 2**20
+        ),
+        cost_estimate=pl.CostEstimate(
+            flops=60 * rows * full, bytes_accessed=6 * rows * full, transcendentals=0
+        ),
+    )(partials.reshape(dims + (full,)), master, moment_one, moment_two)
+    return outs[:4] + (outs[4].reshape(rows, full),)
 
 
 def block_scale(amax):
@@ -52,9 +539,15 @@
     return (master_new, moment_one_new, moment_two_new, reduced_grad, weights)
 
 
+def step_on_device(partials, master, moment_one, moment_two):
+    if lax.axis_size("dp") == 32 and master.shape[0] == 8 and partials.shape[2] == 128 * BLOCK:
+        return fused(partials, master, moment_one, moment_two)
+    return per_device(partials, master, moment_one, moment_two)
+
+
 def solution(mesh):
     in_specs = (P("dp", None, None), P("dp", None), P("dp", None), P("dp", None))
     out_specs = (P("dp", None), P("dp", None), P("dp", None), P("dp", None), P())
     return jax.shard_map(
-        per_device, mesh=mesh, in_specs=in_specs, out_specs=out_specs, check_vma=False
+        step_on_device, mesh=mesh, in_specs=in_specs, out_specs=out_specs, check_vma=False
     )

time: 458 us -> 156 us (0.34)
  waiting for transfers between devices: 383 us -> 0 us
  Pallas kernels: 0 us -> 140 us
  other arithmetic: 38.4 us -> 0 us
  between operations: 13.8 us -> 0.64 us
  local copies, waits for them, and re-layouts: 21.6 us -> 15.1 us
    reduce_scatter x1 -> x0, waiting for transfers between devices: 182 us -> none  [per_device(): total = lax.psum_scatter(mant, 'dp', scatter_dimension=0, tiled=True)]
    pallas_call x0 -> x1, Pallas kernels: none -> 140 us  [fused(): pl.pallas_call(functools.partial(kernel, n, half), out_shape=(state,) * 4...]
    pmax x1 -> x0, waiting for transfers between devices: 122 us -> none  [per_device(): lax.pmax(jnp.max(mags, axis=2).astype(jnp.bfloat16), 'dp')]
    all_gather x1 -> x0, waiting for transfers between devices: 79.3 us -> none  [per_device(): weights = lax.all_gather(own_weights, 'dp', axis=0, tiled=True)]
    floor x1 -> x0, other arithmetic: 17.3 us -> none  [per_device(): mant = jnp.floor(vals + 0.5).reshape(rows, width)]
    reduce_max x3 -> x0, other arithmetic: 9.81 us -> none  [the longest x1 6.37 us: per_device(): jnp.max(mags, axis=2).astype(jnp.bfloat16)]
    unnamed x1 -> x0, other arithmetic: 9.56 us -> none
    mul x1 -> x0, local copies, waits for them, and re-layouts: 4.61 us -> none  [per_device(): local.astype(jnp.float32).reshape(rows, nblk, BLOCK) * mult[:, :, None]]
  transfers between devices with their start and end apart: 3 -> 0, of which waited for: 3 -> 0; matrix products, arithmetic and copies ran while one was open for 0% -> 0% of each run, Pallas kernels for 0% -> 0%
where the time goes in v1:
time: 156 us
  Pallas kernels  140 us (90%)
  local copies, waits for them, and re-layouts  15.1 us (10%)
    pallas_call x1, Pallas kernels, fused(): pl.pallas_call(functools.partial(kernel, n, half), out_shape=(state,) * 4...  140 us
    unnamed x5, local copies, waits for them, and re-layouts  15.1 us

profile of v1, /device:TPU:1, one launch (start us, length us, event | category | flops | bytes accessed | tf_op | source)
XLA Modules:
  0.0 156.0 jit_solution(819383075683283382)
XLA Ops:
  0.6 140.2 %shard_map.83 = (f32[8,16384]{1,0:T(8,128)}, f32[8,16384]{1,0:T(8,128)}, f32[8,16384]{1,0:T(8,128)}, f32[8,16384]{1,0:T(8,128)}, bf16[2,2,2,2,16,16384]{5,4,3,2,1,0:T(8,128)(2,1)}) custom-call(bf16[2,2,2,2,16,16384]{5,4,3,2,1,0:T(8,128)(2,1)} %bitcast.2, f32[8,16384]{1,0:T(8,128)} %master.1, f32[8,16384]{1,0:T(8,128)} %one.1, f32[8,16384]{1,0:T(8,128)} %two.1), custom_call_target="tpu_custom_call" | custom-call | flops 251658240 | bytes 25165824 | tf_op jit(solution)/shard_map/pallas_call | solution.py:443
  140.9 1.9 %copy.14 = f32[8,16384]{1,0:T(8,128)} copy(f32[8,16384]{1,0:T(8,128)} %get-tuple-element.20) | data formatting | bytes 1048576
  142.7 1.9 %copy.15 = f32[8,16384]{1,0:T(8,128)} copy(f32[8,16384]{1,0:T(8,128)} %get-tuple-element.21) | data formatting | bytes 1048576
  144.6 1.9 %copy.16 = f32[8,16384]{1,0:T(8,128)} copy(f32[8,16384]{1,0:T(8,128)} %get-tuple-element.22) | data formatting | bytes 1048576
  146.5 1.9 %copy.17 = f32[8,16384]{1,0:T(8,128)} copy(f32[8,16384]{1,0:T(8,128)} %get-tuple-element.23) | data formatting | bytes 1048576
  148.3 7.7 %copy.18 = bf16[256,16384]{1,0:T(8,128)(2,1)} copy(bf16[256,16384]{1,0:T(8,128)(2,1)} %bitcast.3) | data formatting | bytes 16777216

commit v2 on v1

v2 whole, which is shorter than its diff:
```python
import functools

import jax
import jax.numpy as jnp
from jax import lax
from jax.experimental import pallas as pl
from jax.experimental.pallas import tpu as pltpu
from jax.sharding import PartitionSpec as P

BLOCK = 128
MBITS = 7
STEP = 20
CHUNKS = 8
SWAPS = 4
F32 = jnp.float32
BF16 = jnp.bfloat16


def adam(grad, master, one, two):
    one_new = 0.9 * one + 0.1 * grad
    two_new = 0.95 * two + 0.05 * grad * grad
    first = one_new / (1.0 - 0.9**STEP)
    second = two_new / (1.0 - 0.95**STEP)
    update = first / (jnp.sqrt(second) + 1e-08)
    return master - 0.001 * (update + 0.1 * master), one_new, two_new


def kernel(
    n,
    half,
    parts,
    master,
    one,
    two,
    results,
    weights,
    own,
    peer,
    pair,
    amax,
    top_tx,
    top_rx,
    mult,
    factor,
    quad_rx,
    quad,
    line_rx,
    state,
    fresh,
    gathered,
    load_sem,
    peer_send,
    peer_recv,
    state_sem,
    state_send,
    state_recv,
    top_send,
    top_recv,
    quad_send,
    quad_recv,
    line_send,
    line_recv,
    g_send,
    g_recv,
    out_sem,
    out_send,
    out_recv,
):
    me = lax.axis_index("dp")
    core = me % 2
    x = (me // 2) % 2
    y = (me // 4) % 2
    z0 = (me // 8) % 2
    z1 = me // 16
    chip = me // 2
    other_core = me + 1 - 2 * core
    over_x = me + 2 * (1 - 2 * x)
    over_y = me + 4 * (1 - 2 * y)
    over_xy = over_x + 4 * (1 - 2 * y)
    over_z0 = me + 8 * (1 - 2 * z0)
    over_z1 = me + 16 * (1 - 2 * z1)
    over_z01 = over_z0 + 16 * (1 - 2 * z1)
    plane = (over_x, over_y, over_xy)
    line = (over_z0, over_z1, over_z01)
    plane_spots = ((y, 1 - x), (1 - y, x), (1 - y, 1 - x))
    line_spots = ((z1, 1 - z0), (1 - z1, z0), (1 - z1, 1 - z0))
    width = half // CHUNKS
    nblk = width // BLOCK
    mine = core * half
    theirs = (1 - core) * half
    every = slice(None)

    def remote(src, dst, send, recv, device):
        return pltpu.make_async_remote_copy(
            src_ref=src,
            dst_ref=dst,
            send_sem=send,
            recv_sem=recv,
            device_id=(device,),
            device_id_type=pl.DeviceIdType.MESH,
        )

    def at(start, size=width):
        return pl.ds(pl.multiple_of(start, BLOCK), size)

    def cols(j):
        return pl.ds(j * width, width)

    loads = []
    for j in range(SWAPS):
        size = half // SWAPS
        loads.append(
            pltpu.make_async_copy(
                parts.at[:, :, :, :, :, at(mine + j * size, size)],
                own.at[:, :, :, :, :, pl.ds(j * size, size)],
                load_sem.at[j],
            )
        )
        loads[j].start()

    barrier = pltpu.get_barrier_semaphore()
    for device in (other_core,) + plane + line:
        pl.semaphore_signal(
            barrier, inc=1, device_id=(device,), device_id_type=pl.DeviceIdType.MESH
        )
    pl.semaphore_wait(barrier, 7)

    swaps = []
    for j in range(SWAPS):
        size = half // SWAPS
        swaps.append(
            remote(
                parts.at[:, :, :, :, :, at(theirs + j * size, size)],
                peer.at[:, :, :, :, :, pl.ds(j * size, size)],
                peer_send.at[j],
                peer_recv.at[j],
                other_core,
            )
        )
        swaps[j].start()
    states = []
    for i, ref in enumerate((master, one, two)):
        states.append(
            (
                pltpu.make_async_copy(ref.at[:, at(mine, half)], state.at[i, core], state_sem.at[i]),
                remote(
                    ref.at[:, at(theirs, half)],
                    state.at[i, core],
                    state_send.at[i],
                    state_recv.at[i],
                    other_core,
                ),
            )
        )
        for copy in states[i]:
            copy.start()

    amax[...] = jnp.zeros_like(amax)
    lanes = lax.broadcasted_iota(jnp.int32, (BLOCK, BLOCK), 1)
    subs = lax.broadcasted_iota(jnp.int32, (BLOCK, BLOCK), 0)
    shift = half // BLOCK

    def block_max(i, _):
        for h in range(2):
            best = amax[...]
            for u in range(4):
                b = i * 4 + u
                c = at(b * BLOCK, BLOCK)
                a = jnp.abs(own[h, :, :, :, :, c].reshape(BLOCK, BLOCK).astype(F32))
                p = jnp.abs(peer[h, :, :, :, :, c].reshape(BLOCK, BLOCK).astype(F32))
                m = jnp.max(jnp.maximum(a, p), axis=1, keepdims=True)
                best = jnp.where(lanes == b + h * shift, m, best)
            amax[...] = best
        return 0

    for j in range(SWAPS):
        loads[j].wait()
        swaps[j].wait_recv()
        steps = half // BLOCK // SWAPS // 4
        lax.fori_loop(j * steps, (j + 1) * steps, block_max, 0)

    for r, group in enumerate((plane, line)):
        top_tx[r] = amax[...].astype(BF16)
        copies = [
            remote(
                top_tx.at[r], top_rx.at[r, i], top_send.at[r, i], top_recv.at[r, i], device
            )
            for i, device in enumerate(group)
        ]
        for copy in copies:
            copy.start()
        for i, copy in enumerate(copies):
            copy.wait_recv()
        best = amax[...]
        for i in range(3):
            best = jnp.maximum(best, top_rx[r, i].astype(F32))
        amax[...] = best
        for copy in copies:
            copy.wait_send()

    top = amax[...]
    m = jnp.full((BLOCK, BLOCK), 2.0 ** (MBITS + 20), F32)
    f = jnp.full((BLOCK, BLOCK), 2.0**-20 / (2.0**MBITS * n), F32)
    for k in range(-20, 13):
        hit = top >= 2.0**k
        m = jnp.where(hit, 2.0 ** (MBITS - k - 1), m)
        f = jnp.where(hit, 2.0 ** (k + 1) / (2.0**MBITS * n), f)
    mult[...] = m.astype(BF16)
    factor[...] = f

    def spread(values, lane):
        pick = jnp.where(subs == lane, 1.0, 0.0).astype(BF16)
        return jnp.dot(values, pick, preferred_element_type=F32)

    def block_pair(b, _):
        c = at(b * BLOCK, BLOCK)
        for h in range(2):
            s = spread(mult[...], b + h * shift)
            a = own[h, :, :, :, :, c].reshape(BLOCK, BLOCK).astype(F32)
            p = peer[h, :, :, :, :, c].reshape(BLOCK, BLOCK).astype(F32)
            t = jnp.floor(a * s + 0.5) + jnp.floor(p * s + 0.5)
            pair[h, :, :, :, :, c] = t.astype(BF16).reshape(2, 2, 2, 16, BLOCK)
        return 0

    started = {}

    def start(j, key, copies):
        for copy in copies:
            copy.start()
        started[j, key] = copies

    def arrived(j, key):
        for copy in started[j, key]:
            copy.wait_recv()

    def send_pair(j):
        lax.fori_loop(j * nblk, (j + 1) * nblk, block_pair, 0, unroll=2)
        c = cols(j)
        start(
            j,
            "quad",
            [
                remote(
                    pair.at[:, :, yy, xx, :, c],
                    quad_rx.at[i, :, :, :, c],
                    quad_send.at[j, i],
                    quad_recv.at[j, i],
                    plane[i],
                )
                for i, (yy, xx) in enumerate(plane_spots)
            ],
        )

    def send_quad(j):
        arrived(j, "quad")

        def body(b, _):
            c = at(b * BLOCK, BLOCK)
            t = pair[:, :, y, x, :, c].astype(F32)
            for i in range(3):
                t = t + quad_rx[i, :, :, :, c].astype(F32)
            quad[:, :, :, c] = t
            return 0

        lax.fori_loop(j * nblk, (j + 1) * nblk, body, 0, unroll=2)
        c = cols(j)
        start(
            j,
            "line",
            [
                remote(
                    quad.at[a, b, :, c],
                    line_rx.at[i, :, c],
                    line_send.at[j, i],
                    line_recv.at[j, i],
                    line[i],
                )
                for i, (a, b) in enumerate(line_spots)
            ],
        )

    def gather(j, i, spot, device):
        ref = gathered.at[spot]
        return remote(ref, ref, g_send.at[j, i], g_recv.at[j, i], device)

    def update(j):
        if j == 0:
            for near, far in states:
                near.wait()
                far.wait_recv()
        arrived(j, "line")
        rows = pl.ds(pl.multiple_of((chip % 8) * 16, 16), 16)
        scales = factor[rows, :]

        def body(b, _):
            c = at(b * BLOCK, BLOCK)
            lane = b + (chip // 8) * shift
            near = jnp.where(lanes[:16] == lane, scales, 0.0)
            s = jnp.sum(near, axis=1, keepdims=True)
            t = quad[z1, z0, :, c]
            for i in range(3):
                t = t + line_rx[i, :, c]
            g = (t * s).reshape(2, 8, BLOCK)
            new, m1, m2 = adam(g, state[0, :, :, c], state[1, :, :, c], state[2, :, :, c])
            fresh[0, :, :, c] = new
            fresh[1, :, :, c] = m1
            fresh[2, :, :, c] = m2
            fresh[3, :, :, c] = g
            v = new.reshape(16, BLOCK)
            w = jnp.max(jnp.abs(v), axis=1, keepdims=True) + 1e-06
            v = (v / w).astype(BF16).astype(F32) * w
            gathered[z1, z0, y, x, :, c] = v.astype(BF16)
            return 0

        lax.fori_loop(j * nblk, (j + 1) * nblk, body, 0, unroll=4)
        c = cols(j)
        spot = (z1, z0, y, x, every, c)
        start(j, "g1", [gather(j, i, spot, device) for i, device in enumerate(line)])
        c_out = at(mine + j * width)
        start(
            j,
            "state",
            [
                remote(
                    fresh.at[:, 1 - core, :, c],
                    results.at[:, :, c_out],
                    out_send.at[j, 0],
                    out_recv.at[j, 0],
                    other_core,
                )
            ],
        )
        keep(fresh.at[:, core, :, c], results.at[:, :, c_out], out_sem.at[j, 0])

    kept = []

    def keep(src, dst, sem):
        kept.append(pltpu.make_async_copy(src, dst, sem))
        kept[-1].start()

    def gather_first(j):
        arrived(j, "g1")
        ca = pl.ds(j * width, width // 2)
        cb = pl.ds(j * width + width // 2, width // 2)
        start(
            j,
            "g2",
            [
                gather(j, 3, (every, every, y, x, every, ca), over_y),
                gather(j, 4, (every, every, y, x, every, cb), over_x),
            ],
        )

    def gather_second(j):
        arrived(j, "g2")
        ca = pl.ds(j * width, width // 2)
        cb = pl.ds(j * width + width // 2, width // 2)
        start(
            j,
            "g3",
            [
                gather(j, 5, (every, every, every, x, every, ca), over_x),
                gather(j, 6, (every, every, y, every, every, cb), over_y),
            ],
        )

    def hand_out(j):
        arrived(j, "g3")
        src = gathered.at[:, :, :, :, :, cols(j)]
        dst = weights.at[:, :, :, :, :, at(mine + j * width)]
        start(j, "out", [remote(src, dst, out_send.at[j, 1], out_recv.at[j, 1], other_core)])
        keep(src, dst, out_sem.at[j, 1])

    stages = (send_pair, send_quad, update, gather_first, gather_second, hand_out)
    for t in range(CHUNKS + len(stages) - 1):
        for s in range(len(stages)):
            if 0 <= t - s < CHUNKS:
                stages[s](t - s)
    for j in range(CHUNKS):
        arrived(j, "out")
        arrived(j, "state")
    for copy in kept:
        copy.wait()
    for swap in swaps:
        swap.wait_send()
    for _, far in states:
        far.wait_send()
    for copies in started.values():
        for copy in copies:
            copy.wait_send()


def hand_over(results, weights, master_new, one_new, two_new, grad, out, sem):
    copies = [
        pltpu.make_async_copy(results.at[i], ref, sem.at[16 + i])
        for i, ref in enumerate((master_new, one_new, two_new, grad))
    ]
    for i in range(16):
        spot = (i // 8, i // 4 % 2, i // 2 % 2, i % 2)
        copies.append(pltpu.make_async_copy(weights.at[spot], out.at[spot], sem.at[i]))
    for copy in copies:
        copy.start()
    for copy in copies:
        copy.wait()


def fused(partials, master, moment_one, moment_two):
    n = lax.axis_size("dp")
    rows, full = partials.shape[1:]
    half = full // 2
    dims = (2, 2, 2, 2, 16)
    hbm = pl.BlockSpec(memory_space=pl.ANY)
    slab = jax.ShapeDtypeStruct(dims + (full,), BF16)
    dma = pltpu.SemaphoreType.DMA
    results, weights = pl.pallas_call(
        functools.partial(kernel, n, half),
        out_shape=(jax.ShapeDtypeStruct((4,) + master.shape, F32), slab),
        in_specs=[hbm] * 4,
        out_specs=(hbm, hbm),
        scratch_shapes=[
            pltpu.VMEM(dims + (half,), BF16),
            pltpu.VMEM(dims + (half,), BF16),
            pltpu.VMEM(dims + (half,), BF16),
            pltpu.VMEM((BLOCK, BLOCK), F32),
            pltpu.VMEM((2, BLOCK, BLOCK), BF16),
            pltpu.VMEM((2, 3, BLOCK, BLOCK), BF16),
            pltpu.VMEM((BLOCK, BLOCK), BF16),
            pltpu.VMEM((BLOCK, BLOCK), F32),
            pltpu.VMEM((3, 2, 2, 16, half), BF16),
            pltpu.VMEM((2, 2, 16, half), F32),
            pltpu.VMEM((3, 16, half), F32),
            pltpu.VMEM((3, 2, 8, half), F32),
            pltpu.VMEM((4, 2, 8, half), F32),
            pltpu.VMEM(dims + (half,), BF16),
            dma((SWAPS,)),
            dma((SWAPS,)),
            dma((SWAPS,)),
            dma((3,)),
            dma((3,)),
            dma((3,)),
            dma((2, 3)),
            dma((2, 3)),
            dma((CHUNKS, 3)),
            dma((CHUNKS, 3)),
            dma((CHUNKS, 3)),
            dma((CHUNKS, 3)),
            dma((CHUNKS, 7)),
            dma((CHUNKS, 7)),
            dma((CHUNKS, 2)),
            dma((CHUNKS, 2)),
            dma((CHUNKS, 2)),
        ],
        compiler_params=pltpu.CompilerParams(
            collective_id=0, has_side_effects=True, vmem_limit_bytes=56 * 2**20
        ),
        cost_estimate=pl.CostEstimate(
            flops=60 * rows * full, bytes_accessed=6 * rows * full, transcendentals=0
        ),
    )(partials.reshape(dims + (full,)), master, moment_one, moment_two)
    outs = pl.pallas_call(
        hand_over,
        out_shape=(jax.ShapeDtypeStruct(master.shape, F32),) * 4 + (slab,),
        in_specs=[hbm] * 2,
        out_specs=(hbm,) * 5,
        scratch_shapes=[dma((20,))],
        cost_estimate=pl.CostEstimate(
            flops=0, bytes_accessed=5 * rows * full, transcendentals=0
        ),
    )(results, weights)
    return outs[:4] + (outs[4].reshape(rows, full),)


def block_scale(amax):
    powers = jnp.asarray([2.0**k for k in range(-20, 13)], jnp.float32)
    doubled = jnp.asarray([2.0 ** (k + 1) for k in range(-20, 13)], jnp.float32)
    inverse = jnp.asarray([2.0 ** (MBITS - k - 1) for k in range(-20, 13)], jnp.float32)
    hit = amax[..., None] >= powers
    scale = jnp.max(jnp.where(hit, doubled, jnp.float32(2.0 ** (-20))), axis=-1)
    mult = jnp.min(jnp.where(hit, inverse, jnp.float32(2.0 ** (MBITS + 20))), axis=-1)
    return (scale, mult)


def per_device(partials, master, moment_one, moment_two):
    devices = lax.axis_size("dp")
    local = partials[0]
    rows = local.shape[0]
    width = local.shape[1]
    nblk = width // BLOCK
    owned = master.shape[0]
    mags = jnp.abs(local.astype(jnp.float32)).reshape(rows, nblk, BLOCK)
    shared = lax.pmax(jnp.max(mags, axis=2).astype(jnp.bfloat16), "dp").astype(jnp.float32)
    scale_all, mult = block_scale(shared)
    vals = local.astype(jnp.float32).reshape(rows, nblk, BLOCK) * mult[:, :, None]
    mant = jnp.floor(vals + 0.5).reshape(rows, width)
    total = lax.psum_scatter(mant, "dp", scatter_dimension=0, tiled=True)
    start = lax.axis_index("dp") * owned
    scale = lax.dynamic_slice_in_dim(scale_all, start, owned, 0)
    total = total.reshape(owned, nblk, BLOCK)
    factor = scale / (2.0**MBITS * devices)
    reduced_grad = (total * factor[:, :, None]).reshape(owned, width)
    moment_one_new = 0.9 * moment_one + 0.1 * reduced_grad
    moment_two_new = 0.95 * moment_two + 0.05 * reduced_grad * reduced_grad
    first = moment_one_new / (1.0 - 0.9**STEP)
    second = moment_two_new / (1.0 - 0.95**STEP)
    update = first / (jnp.sqrt(second) + 1e-08)
    master_new = master - 0.001 * (update + 0.1 * master)
    blocks = master_new.reshape(owned, nblk, BLOCK)
    wscale = jnp.max(jnp.abs(blocks), axis=2) + 1e-06
    wmant = (blocks / wscale[:, :, None]).astype(jnp.bfloat16)
    own_weights = (
        (wmant.astype(jnp.float32) * wscale[:, :, None]).reshape(owned, width).astype(jnp.bfloat16)
    )
    weights = lax.all_gather(own_weights, "dp", axis=0, tiled=True)
    return (master_new, moment_one_new, moment_two_new, reduced_grad, weights)


def step_on_device(partials, master, moment_one, moment_two):
    if lax.axis_size("dp") == 32 and master.shape[0] == 8 and partials.shape[2] == 128 * BLOCK:
        return fused(partials, master, moment_one, moment_two)
    return per_device(partials, master, moment_one, moment_two)


def solution(mesh):
    in_specs = (P("dp", None, None), P("dp", None), P("dp", None), P("dp", None))
    out_specs = (P("dp", None), P("dp", None), P("dp", None), P("dp", None), P())
    return jax.shard_map(
        step_on_device, mesh=mesh, in_specs=in_specs, out_specs=out_specs, check_vma=False
    )
```

time: 156 us -> 435 us (2.79)
  Pallas kernels: 140 us -> 434 us
  local copies, waits for them, and re-layouts: 15.1 us -> 0 us
    pallas_call x1 -> x2, Pallas kernels: 140 us -> 434 us  [the longest x1 319 us: fused(): pl.pallas_call(hand_over, out_shape=(jax.ShapeDtypeStruct(master.shape, F...]
    unnamed x5 -> x0, local copies, waits for them, and re-layouts: 15.1 us -> none
where the time goes in v2:
time: 435 us
  Pallas kernels  434 us (100%)
    pallas_call x1, Pallas kernels, fused(): pl.pallas_call(hand_over, out_shape=(jax.ShapeDtypeStruct(master.shape, F...  319 us
    pallas_call x1, Pallas kernels, fused(): pl.pallas_call(functools.partial(kernel, n, half), out_shape=(jax.ShapeDt...  115 us

profile of v2, /device:TPU:1, one launch (start us, length us, event | category | flops | bytes accessed | tf_op | source)
XLA Modules:
  0.0 435.0 jit_solution(9931069258512015355)
XLA Ops:
  0.6 115.5 %shard_map.83 = (f32[4,8,16384]{2,1,0:T(8,128)}, bf16[2,2,2,2,16,16384]{5,4,3,2,1,0:T(8,128)(2,1)}) custom-call(bf16[2,2,2,2,16,16384]{5,4,3,2,1,0:T(8,128)(2,1)} %bitcast.2, f32[8,16384]{1,0:T(8,128)} %master.1, f32[8,16384]{1,0:T(8,128)} %one.1, f32[8,16384]{1,0:T(8,128)} %two.1), custom_call_target="tpu_custom_call" | custom-call | flops 251658240 | bytes 25165824 | tf_op jit(solution)/shard_map/pallas_call | solution.py:415
  116.1 318.9 %shard_map.84 = (f32[8,16384]{1,0:T(8,128)}, f32[8,16384]{1,0:T(8,128)}, f32[8,16384]{1,0:T(8,128)}, f32[8,16384]{1,0:T(8,128)}, bf16[2,2,2,2,16,16384]{5,4,3,2,1,0:T(8,128)(2,1)}) custom-call(f32[4,8,16384]{2,1,0:T(8,128)} %get-tuple-element.12.results, bf16[2,2,2,2,16,16384]{5,4,3,2,1,0:T(8,128)(2,1)} %get-tuple-element.13.weights), custom_call_target="tpu_custom_call" | custom-call | bytes 20971520 | tf_op jit(solution)/shard_map/pallas_call | solution.py:460

commit v3 on v2

--- a/solution.py
+++ b/solution.py
@@ -23,6 +23,18 @@
     second = two_new / (1.0 - 0.95**STEP)
     update = first / (jnp.sqrt(second) + 1e-08)
     return master - 0.001 * (update + 0.1 * master), one_new, two_new
+
+
+def encode(total):
+    odd = total - 2.0 * jnp.floor(total * 0.5) > 0.5
+    wide = jnp.where(odd, (total - 1.0) * 2.0**20, total * 2.0**10)
+    return jnp.where(jnp.abs(total) <= 256.0, total, wide).astype(BF16)
+
+
+def decode(code):
+    size = jnp.abs(code)
+    wide = jnp.where(size > 2.0**19, code * 2.0**-20 + 1.0, code * 2.0**-10)
+    return jnp.where(size <= 256.0, code, wide)
 
 
 def kernel(
@@ -42,6 +54,8 @@
     top_rx,
     mult,
     factor,
+    half_rx,
+    half_tx,
     quad_rx,
     quad,
     line_rx,
@@ -56,6 +70,8 @@
     state_recv,
     top_send,
     top_recv,
+    half_send,
+    half_recv,
     quad_send,
     quad_recv,
     line_send,
@@ -82,7 +98,6 @@
     over_z01 = over_z0 + 16 * (1 - 2 * z1)
     plane = (over_x, over_y, over_xy)
     line = (over_z0, over_z1, over_z01)
-    plane_spots = ((y, 1 - x), (1 - y, x), (1 - y, 1 - x))
     line_spots = ((z1, 1 - z0), (1 - z1, z0), (1 - z1, 1 - z0))
     width = half // CHUNKS
     nblk = width // BLOCK
@@ -160,9 +175,9 @@
     subs = lax.broadcasted_iota(jnp.int32, (BLOCK, BLOCK), 0)
     shift = half // BLOCK
 
-    def block_max(i, _):
+    def block_max(g, i):
         for h in range(2):
-            best = amax[...]
+            best = amax[g]
             for u in range(4):
                 b = i * 4 + u
                 c = at(b * BLOCK, BLOCK)
@@ -170,57 +185,72 @@
                 p = jnp.abs(peer[h, :, :, :, :, c].reshape(BLOCK, BLOCK).astype(F32))
                 m = jnp.max(jnp.maximum(a, p), axis=1, keepdims=True)
                 best = jnp.where(lanes == b + h * shift, m, best)
-            amax[...] = best
-        return 0
-
-    for j in range(SWAPS):
+            amax[g] = best
+
+    def find_max(j):
         loads[j].wait()
         swaps[j].wait_recv()
         steps = half // BLOCK // SWAPS // 4
-        lax.fori_loop(j * steps, (j + 1) * steps, block_max, 0)
-
-    for r, group in enumerate((plane, line)):
-        top_tx[r] = amax[...].astype(BF16)
-        copies = [
+
+        def body(i, _):
+            block_max(min(j, 1), i)
+            return 0
+
+        lax.fori_loop(j * steps, (j + 1) * steps, body, 0)
+
+    tops = {}
+
+    def send_top(g, r):
+        top_tx[g, r] = amax[g].astype(BF16)
+        tops[g, r] = [
             remote(
-                top_tx.at[r], top_rx.at[r, i], top_send.at[r, i], top_recv.at[r, i], device
+                top_tx.at[g, r],
+                top_rx.at[g, r, i],
+                top_send.at[g, r, i],
+                top_recv.at[g, r, i],
+                device,
             )
-            for i, device in enumerate(group)
+            for i, device in enumerate((plane, line)[r])
         ]
-        for copy in copies:
+        for copy in tops[g, r]:
             copy.start()
-        for i, copy in enumerate(copies):
+
+    def take_top(g, r):
+        for copy in tops[g, r]:
             copy.wait_recv()
-        best = amax[...]
+        best = amax[g]
         for i in range(3):
-            best = jnp.maximum(best, top_rx[r, i].astype(F32))
-        amax[...] = best
-        for copy in copies:
-            copy.wait_send()
-
-    top = amax[...]
-    m = jnp.full((BLOCK, BLOCK), 2.0 ** (MBITS + 20), F32)
-    f = jnp.full((BLOCK, BLOCK), 2.0**-20 / (2.0**MBITS * n), F32)
-    for k in range(-20, 13):
-        hit = top >= 2.0**k
-        m = jnp.where(hit, 2.0 ** (MBITS - k - 1), m)
-        f = jnp.where(hit, 2.0 ** (k + 1) / (2.0**MBITS * n), f)
-    mult[...] = m.astype(BF16)
-    factor[...] = f
+            best = jnp.maximum(best, top_rx[g, r, i].astype(F32))
+        amax[g] = best
+
+    def find_scales(g):
+        top = amax[g]
+        m = jnp.full((BLOCK, BLOCK), 2.0 ** (MBITS + 20), F32)
+        f = jnp.full((BLOCK, BLOCK), 2.0**-20 / (2.0**MBITS * n), F32)
+        for k in range(-20, 13):
+            hit = top >= 2.0**k
+            m = jnp.where(hit, 2.0 ** (MBITS - k - 1), m)
+            f = jnp.where(hit, 2.0 ** (k + 1) / (2.0**MBITS * n), f)
+        mult[g] = m.astype(BF16)
+        factor[g] = f
 
     def spread(values, lane):
         pick = jnp.where(subs == lane, 1.0, 0.0).astype(BF16)
         return jnp.dot(values, pick, preferred_element_type=F32)
 
-    def block_pair(b, _):
+    def block_pair(g, b):
         c = at(b * BLOCK, BLOCK)
         for h in range(2):
-            s = spread(mult[...], b + h * shift)
+            s = spread(mult[g], b + h * shift)
             a = own[h, :, :, :, :, c].reshape(BLOCK, BLOCK).astype(F32)
             p = peer[h, :, :, :, :, c].reshape(BLOCK, BLOCK).astype(F32)
             t = jnp.floor(a * s + 0.5) + jnp.floor(p * s + 0.5)
             pair[h, :, :, :, :, c] = t.astype(BF16).reshape(2, 2, 2, 16, BLOCK)
-        return 0
+
+    early = CHUNKS // SWAPS
+
+    def group(j):
+        return 0 if j < early else 1
 
     started = {}
 
@@ -233,21 +263,74 @@
         for copy in started[j, key]:
             copy.wait_recv()
 
+    def streams(j):
+        return (
+            pl.ds(j * width, width // 2),
+            pl.ds(j * width + width // 2, width // 2),
+        )
+
     def send_pair(j):
-        lax.fori_loop(j * nblk, (j + 1) * nblk, block_pair, 0, unroll=2)
-        c = cols(j)
+        def body(b, _):
+            block_pair(group(j), b)
+            return 0
+
+        lax.fori_loop(j * nblk, (j + 1) * nblk, body, 0, unroll=2)
+        ca, cb = streams(j)
+        start(
+            j,
+            "half",
+            [
+                remote(
+                    pair.at[:, :, :, 1 - x, :, ca],
+                    half_rx.at[:, :, :, :, ca],
+                    half_send.at[j, 0],
+                    half_recv.at[j, 0],
+                    over_x,
+                ),
+                remote(
+                    pair.at[:, :, 1 - y, :, :, cb],
+                    half_rx.at[:, :, :, :, cb],
+                    half_send.at[j, 1],
+                    half_recv.at[j, 1],
+                    over_y,
+                ),
+            ],
+        )
+
+    def send_half(j):
+        arrived(j, "half")
+
+        def first(b, _):
+            c = at(b * BLOCK, BLOCK)
+            near = pair[:, :, y, x, :, c].astype(F32) + half_rx[:, :, y, :, c].astype(F32)
+            far = pair[:, :, 1 - y, x, :, c].astype(F32) + half_rx[:, :, 1 - y, :, c].astype(F32)
+            quad[:, :, :, c] = near
+            half_tx[:, :, :, c] = encode(far)
+            return 0
+
+        def second(b, _):
+            c = at(b * BLOCK, BLOCK)
+            near = pair[:, :, y, x, :, c].astype(F32) + half_rx[:, :, x, :, c].astype(F32)
+            far = pair[:, :, y, 1 - x, :, c].astype(F32) + half_rx[:, :, 1 - x, :, c].astype(F32)
+            quad[:, :, :, c] = near
+            half_tx[:, :, :, c] = encode(far)
+            return 0
+
+        middle = j * nblk + nblk // 2
+        lax.fori_loop(j * nblk, middle, first, 0, unroll=2)
+        lax.fori_loop(middle, (j + 1) * nblk, second, 0, unroll=2)
         start(
             j,
             "quad",
             [
                 remote(
-                    pair.at[:, :, yy, xx, :, c],
-                    quad_rx.at[i, :, :, :, c],
+                    half_tx.at[:, :, :, c],
+                    quad_rx.at[:, :, :, c],
                     quad_send.at[j, i],
                     quad_recv.at[j, i],
-                    plane[i],
+                    device,
                 )
-                for i, (yy, xx) in enumerate(plane_spots)
+                for i, (c, device) in enumerate(zip(streams(j), (over_y, over_x)))
             ],
         )
 
@@ -256,10 +339,7 @@
 
         def body(b, _):
             c = at(b * BLOCK, BLOCK)
-            t = pair[:, :, y, x, :, c].astype(F32)
-            for i in range(3):
-                t = t + quad_rx[i, :, :, :, c].astype(F32)
-            quad[:, :, :, c] = t
+            quad[:, :, :, c] = quad[:, :, :, c] + decode(quad_rx[:, :, :, c].astype(F32))
             return 0
 
         lax.fori_loop(j * nblk, (j + 1) * nblk, body, 0, unroll=2)
@@ -290,7 +370,7 @@
                 far.wait_recv()
         arrived(j, "line")
         rows = pl.ds(pl.multiple_of((chip % 8) * 16, 16), 16)
-        scales = factor[rows, :]
+        scales = factor[group(j), rows, :]
 
         def body(b, _):
             c = at(b * BLOCK, BLOCK)
@@ -340,8 +420,7 @@
 
     def gather_first(j):
         arrived(j, "g1")
-        ca = pl.ds(j * width, width // 2)
-        cb = pl.ds(j * width + width // 2, width // 2)
+        ca, cb = streams(j)
         start(
             j,
             "g2",
@@ -353,8 +432,7 @@
 
     def gather_second(j):
         arrived(j, "g2")
-        ca = pl.ds(j * width, width // 2)
-        cb = pl.ds(j * width + width // 2, width // 2)
+        ca, cb = streams(j)
         start(
             j,
             "g3",
@@ -371,11 +449,29 @@
         start(j, "out", [remote(src, dst, out_send.at[j, 1], out_recv.at[j, 1], other_core)])
         keep(src, dst, out_sem.at[j, 1])
 
-    stages = (send_pair, send_quad, update, gather_first, gather_second, hand_out)
+    find_max(0)
+    send_top(0, 0)
+    find_max(1)
+    take_top(0, 0)
+    send_top(0, 1)
+    find_max(2)
+    take_top(0, 1)
+    find_scales(0)
+
+    stages = (send_pair, send_half, send_quad, update, gather_first, gather_second, hand_out)
     for t in range(CHUNKS + len(stages) - 1):
+        if t == early - 1:
+            find_max(3)
+            send_top(1, 0)
+        if t == early:
+            take_top(1, 1)
+            find_scales(1)
         for s in range(len(stages)):
             if 0 <= t - s < CHUNKS:
                 stages[s](t - s)
+            if s == 0 and t == early - 1:
+                take_top(1, 0)
+                send_top(1, 1)
     for j in range(CHUNKS):
         arrived(j, "out")
         arrived(j, "state")
@@ -383,6 +479,9 @@
         copy.wait()
     for swap in swaps:
         swap.wait_send()
+    for copies in tops.values():
+        for copy in copies:
+            copy.wait_send()
     for _, far in states:
         far.wait_send()
     for copies in started.values():
@@ -390,18 +489,26 @@
             copy.wait_send()
 
 
-def hand_over(results, weights, master_new, one_new, two_new, grad, out, sem):
-    copies = [
-        pltpu.make_async_copy(results.at[i], ref, sem.at[16 + i])
-        for i, ref in enumerate((master_new, one_new, two_new, grad))
-    ]
+def hand_over(results, weights, master_new, one_new, two_new, grad, out, state, slab, sem_in, sem_out):
+    copies = []
+    for i, ref in enumerate((master_new, one_new, two_new, grad)):
+        copies.append((results.at[i], state.at[i], ref))
     for i in range(16):
         spot = (i // 8, i // 4 % 2, i // 2 % 2, i % 2)
-        copies.append(pltpu.make_async_copy(weights.at[spot], out.at[spot], sem.at[i]))
-    for copy in copies:
-        copy.start()
-    for copy in copies:
-        copy.wait()
+        copies.append((weights.at[spot], slab.at[spot], out.at[spot]))
+    reads = [
+        pltpu.make_async_copy(src, mid, sem_in.at[i]) for i, (src, mid, _) in enumerate(copies)
+    ]
+    writes = [
+        pltpu.make_async_copy(mid, dst, sem_out.at[i]) for i, (_, mid, dst) in enumerate(copies)
+    ]
+    for read in reads:
+        read.start()
+    for read, write in zip(reads, writes):
+        read.wait()
+        write.start()
+    for write in writes:
+        write.wait()
 
 
 def fused(partials, master, moment_one, moment_two):
@@ -421,12 +528,14 @@
             pltpu.VMEM(dims + (half,), BF16),
             pltpu.VMEM(dims + (half,), BF16),
             pltpu.VMEM(dims + (half,), BF16),
-            pltpu.VMEM((BLOCK, BLOCK), F32),
+            pltpu.VMEM((2, BLOCK, BLOCK), F32),
+            pltpu.VMEM((2, 2, BLOCK, BLOCK), BF16),
+            pltpu.VMEM((2, 2, 3, BLOCK, BLOCK), BF16),
             pltpu.VMEM((2, BLOCK, BLOCK), BF16),
-            pltpu.VMEM((2, 3, BLOCK, BLOCK), BF16),
-            pltpu.VMEM((BLOCK, BLOCK), BF16),
-            pltpu.VMEM((BLOCK, BLOCK), F32),
-            pltpu.VMEM((3, 2, 2, 16, half), BF16),
+            pltpu.VMEM((2, BLOCK, BLOCK), F32),
+            pltpu.VMEM((2, 2, 2, 16, half), BF16),
+            pltpu.VMEM((2, 2, 16, half), BF16),
+            pltpu.VMEM((2, 2, 16, half), BF16),
             pltpu.VMEM((2, 2, 16, half), F32),
             pltpu.VMEM((3, 16, half), F32),
             pltpu.VMEM((3, 2, 8, half), F32),
@@ -438,10 +547,12 @@
             dma((3,)),
             dma((3,)),
             dma((3,)),
-            dma((2, 3)),
-            dma((2, 3)),
-            dma((CHUNKS, 3)),
-            dma((CHUNKS, 3)),
+            dma((2, 2, 3)),
+            dma((2, 2, 3)),
+            dma((CHUNKS, 2)),
+            dma((CHUNKS, 2)),
+            dma((CHUNKS, 2)),
+            dma((CHUNKS, 2)),
             dma((CHUNKS, 3)),
             dma((CHUNKS, 3)),
             dma((CHUNKS, 7)),
@@ -462,7 +573,13 @@
         out_shape=(jax.ShapeDtypeStruct(master.shape, F32),) * 4 + (slab,),
         in_specs=[hbm] * 2,
         out_specs=(hbm,) * 5,
-        scratch_shapes=[dma((20,))],
+        scratch_shapes=[
+            pltpu.VMEM((4,) + master.shape, F32),
+            pltpu.VMEM(dims + (full,), BF16),
+            dma((20,)),
+            dma((20,)),
+        ],
+        compiler_params=pltpu.CompilerParams(vmem_limit_bytes=56 * 2**20),
         cost_estimate=pl.CostEstimate(
             flops=0, bytes_accessed=5 * rows * full, transcendentals=0
         ),

time: 435 us -> 121 us (0.28)
  Pallas kernels: 434 us -> 120 us
    pallas_call x1, Pallas kernels: 319 us -> 8.03 us  [fused(): pl.pallas_call(hand_over, out_shape=(jax.ShapeDtypeStruct(master.shape, F...]
where the time goes in v3:
time: 121 us
  Pallas kernels  120 us (99%)
    pallas_call x1, Pallas kernels, fused(): pl.pallas_call(functools.partial(kernel, n, half), out_shape=(jax.ShapeDt...  112 us
    pallas_call x1, Pallas kernels, fused(): pl.pallas_call(hand_over, out_shape=(jax.ShapeDtypeStruct(master.shape, F...  8.03 us

profile of v3, /device:TPU:1, one launch (start us, length us, event | category | flops | bytes accessed | tf_op | source)
XLA Modules:
  0.0 121.0 jit_solution(3056860872836315749)
XLA Ops:
  0.6 112.3 %shard_map.83 = (f32[4,8,16384]{2,1,0:T(8,128)}, bf16[2,2,2,2,16,16384]{5,4,3,2,1,0:T(8,128)(2,1)}) custom-call(bf16[2,2,2,2,16,16384]{5,4,3,2,1,0:T(8,128)(2,1)} %bitcast.2, f32[8,16384]{1,0:T(8,128)} %master.1, f32[8,16384]{1,0:T(8,128)} %one.1, f32[8,16384]{1,0:T(8,128)} %two.1), custom_call_target="tpu_custom_call" | custom-call | flops 251658240 | bytes 25165824 | tf_op jit(solution)/shard_map/pallas_call | solution.py:522
  113.0 8.0 %shard_map.84 = (f32[8,16384]{1,0:T(8,128)}, f32[8,16384]{1,0:T(8,128)}, f32[8,16384]{1,0:T(8,128)}, f32[8,16384]{1,0:T(8,128)}, bf16[2,2,2,2,16,16384]{5,4,3,2,1,0:T(8,128)(2,1)}) custom-call(f32[4,8,16384]{2,1,0:T(8,128)} %get-tuple-element.12.results, bf16[2,2,2,2,16,16384]{5,4,3,2,1,0:T(8,128)(2,1)} %get-tuple-element.13.weights), custom_call_target="tpu_custom_call" | custom-call | bytes 20971520 | tf_op jit(solution)/shard_map/pallas_call | solution.py:571

commit v4 on v3

--- a/solution.py
+++ b/solution.py
@@ -10,7 +10,8 @@
 BLOCK = 128
 MBITS = 7
 STEP = 20
-CHUNKS = 8
+WIDTHS = (8, 8, 12, 12, 8, 8, 4, 4)
+CHUNKS = len(WIDTHS)
 SWAPS = 4
 F32 = jnp.float32
 BF16 = jnp.bfloat16
@@ -25,16 +26,20 @@
     return master - 0.001 * (update + 0.1 * master), one_new, two_new
 
 
-def encode(total):
-    odd = total - 2.0 * jnp.floor(total * 0.5) > 0.5
-    wide = jnp.where(odd, (total - 1.0) * 2.0**20, total * 2.0**10)
-    return jnp.where(jnp.abs(total) <= 256.0, total, wide).astype(BF16)
-
-
-def decode(code):
+def encode(total, step):
+    rest = total - step * jnp.floor(total * (1.0 / step))
+    scale = jnp.full_like(total, 2.0**10)
+    for r in range(1, step):
+        scale = jnp.where(rest > r - 0.5, 2.0 ** (10 * r + 10), scale)
+    return jnp.where(jnp.abs(total) <= 256.0, total, (total - rest) * scale).astype(BF16)
+
+
+def decode(code, step):
     size = jnp.abs(code)
-    wide = jnp.where(size > 2.0**19, code * 2.0**-20 + 1.0, code * 2.0**-10)
-    return jnp.where(size <= 256.0, code, wide)
+    total = code
+    for r in range(step):
+        total = jnp.where(size > 2.0 ** (10 * r + 14), code * 2.0 ** (-10 * r - 10) + r, total)
+    return total
 
 
 def kernel(
@@ -58,6 +63,7 @@
     half_tx,
     quad_rx,
     quad,
+    line_tx,
     line_rx,
     state,
     fresh,
@@ -99,8 +105,7 @@
     plane = (over_x, over_y, over_xy)
     line = (over_z0, over_z1, over_z01)
     line_spots = ((z1, 1 - z0), (1 - z1, z0), (1 - z1, 1 - z0))
-    width = half // CHUNKS
-    nblk = width // BLOCK
+    first_block = [sum(WIDTHS[:j]) for j in range(CHUNKS + 1)]
     mine = core * half
     theirs = (1 - core) * half
     every = slice(None)
@@ -115,11 +120,14 @@
             device_id_type=pl.DeviceIdType.MESH,
         )
 
-    def at(start, size=width):
+    def at(start, size):
         return pl.ds(pl.multiple_of(start, BLOCK), size)
 
     def cols(j):
-        return pl.ds(j * width, width)
+        return pl.ds(first_block[j] * BLOCK, WIDTHS[j] * BLOCK)
+
+    def cols_out(j):
+        return at(mine + first_block[j] * BLOCK, WIDTHS[j] * BLOCK)
 
     loads = []
     for j in range(SWAPS):
@@ -181,9 +189,9 @@
             for u in range(4):
                 b = i * 4 + u
                 c = at(b * BLOCK, BLOCK)
-                a = jnp.abs(own[h, :, :, :, :, c].reshape(BLOCK, BLOCK).astype(F32))
-                p = jnp.abs(peer[h, :, :, :, :, c].reshape(BLOCK, BLOCK).astype(F32))
-                m = jnp.max(jnp.maximum(a, p), axis=1, keepdims=True)
+                a = jnp.abs(own[h, :, :, :, :, c].reshape(BLOCK, BLOCK))
+                p = jnp.abs(peer[h, :, :, :, :, c].reshape(BLOCK, BLOCK))
+                m = jnp.max(jnp.maximum(a, p).astype(F32), axis=1, keepdims=True)
                 best = jnp.where(lanes == b + h * shift, m, best)
             amax[g] = best
 
@@ -247,7 +255,7 @@
             t = jnp.floor(a * s + 0.5) + jnp.floor(p * s + 0.5)
             pair[h, :, :, :, :, c] = t.astype(BF16).reshape(2, 2, 2, 16, BLOCK)
 
-    early = CHUNKS // SWAPS
+    early = 2
 
     def group(j):
         return 0 if j < early else 1
@@ -264,17 +272,16 @@
             copy.wait_recv()
 
     def streams(j):
-        return (
-            pl.ds(j * width, width // 2),
-            pl.ds(j * width + width // 2, width // 2),
-        )
+        size = WIDTHS[j] * BLOCK // 2
+        start = first_block[j] * BLOCK
+        return pl.ds(start, size), pl.ds(start + size, size)
 
     def send_pair(j):
         def body(b, _):
             block_pair(group(j), b)
             return 0
 
-        lax.fori_loop(j * nblk, (j + 1) * nblk, body, 0, unroll=2)
+        lax.fori_loop(first_block[j], first_block[j + 1], body, 0, unroll=2)
         ca, cb = streams(j)
         start(
             j,
@@ -305,7 +312,7 @@
             near = pair[:, :, y, x, :, c].astype(F32) + half_rx[:, :, y, :, c].astype(F32)
             far = pair[:, :, 1 - y, x, :, c].astype(F32) + half_rx[:, :, 1 - y, :, c].astype(F32)
             quad[:, :, :, c] = near
-            half_tx[:, :, :, c] = encode(far)
+            half_tx[:, :, :, c] = encode(far, 2)
             return 0
 
         def second(b, _):
@@ -313,12 +320,12 @@
             near = pair[:, :, y, x, :, c].astype(F32) + half_rx[:, :, x, :, c].astype(F32)
             far = pair[:, :, y, 1 - x, :, c].astype(F32) + half_rx[:, :, 1 - x, :, c].astype(F32)
             quad[:, :, :, c] = near
-            half_tx[:, :, :, c] = encode(far)
+            half_tx[:, :, :, c] = encode(far, 2)
             return 0
 
-        middle = j * nblk + nblk // 2
-        lax.fori_loop(j * nblk, middle, first, 0, unroll=2)
-        lax.fori_loop(middle, (j + 1) * nblk, second, 0, unroll=2)
+        middle = first_block[j] + WIDTHS[j] // 2
+        lax.fori_loop(first_block[j], middle, first, 0, unroll=2)
+        lax.fori_loop(middle, first_block[j + 1], second, 0, unroll=2)
         start(
             j,
             "quad",
@@ -339,17 +346,19 @@
 
         def body(b, _):
             c = at(b * BLOCK, BLOCK)
-            quad[:, :, :, c] = quad[:, :, :, c] + decode(quad_rx[:, :, :, c].astype(F32))
+            total = quad[:, :, :, c] + decode(quad_rx[:, :, :, c].astype(F32), 2)
+            quad[:, :, :, c] = total
+            line_tx[:, :, :, c] = encode(total, 4)
             return 0
 
-        lax.fori_loop(j * nblk, (j + 1) * nblk, body, 0, unroll=2)
+        lax.fori_loop(first_block[j], first_block[j + 1], body, 0, unroll=2)
         c = cols(j)
         start(
             j,
             "line",
             [
                 remote(
-                    quad.at[a, b, :, c],
+                    line_tx.at[a, b, :, c],
                     line_rx.at[i, :, c],
                     line_send.at[j, i],
                     line_recv.at[j, i],
@@ -379,7 +388,7 @@
             s = jnp.sum(near, axis=1, keepdims=True)
             t = quad[z1, z0, :, c]
             for i in range(3):
-                t = t + line_rx[i, :, c]
+                t = t + decode(line_rx[i, :, c].astype(F32), 4)
             g = (t * s).reshape(2, 8, BLOCK)
             new, m1, m2 = adam(g, state[0, :, :, c], state[1, :, :, c], state[2, :, :, c])
             fresh[0, :, :, c] = new
@@ -392,11 +401,11 @@
             gathered[z1, z0, y, x, :, c] = v.astype(BF16)
             return 0
 
-        lax.fori_loop(j * nblk, (j + 1) * nblk, body, 0, unroll=4)
+        lax.fori_loop(first_block[j], first_block[j + 1], body, 0, unroll=4)
         c = cols(j)
+        c_out = cols_out(j)
         spot = (z1, z0, y, x, every, c)
         start(j, "g1", [gather(j, i, spot, device) for i, device in enumerate(line)])
-        c_out = at(mine + j * width)
         start(
             j,
             "state",
@@ -445,7 +454,7 @@
     def hand_out(j):
         arrived(j, "g3")
         src = gathered.at[:, :, :, :, :, cols(j)]
-        dst = weights.at[:, :, :, :, :, at(mine + j * width)]
+        dst = weights.at[:, :, :, :, :, cols_out(j)]
         start(j, "out", [remote(src, dst, out_send.at[j, 1], out_recv.at[j, 1], other_core)])
         keep(src, dst, out_sem.at[j, 1])
 
@@ -489,26 +498,17 @@
             copy.wait_send()
 
 
-def hand_over(results, weights, master_new, one_new, two_new, grad, out, state, slab, sem_in, sem_out):
+def hand_over(results, weights, master_new, one_new, two_new, grad, out, sem):
     copies = []
-    for i, ref in enumerate((master_new, one_new, two_new, grad)):
-        copies.append((results.at[i], state.at[i], ref))
     for i in range(16):
         spot = (i // 8, i // 4 % 2, i // 2 % 2, i % 2)
-        copies.append((weights.at[spot], slab.at[spot], out.at[spot]))
-    reads = [
-        pltpu.make_async_copy(src, mid, sem_in.at[i]) for i, (src, mid, _) in enumerate(copies)
-    ]
-    writes = [
-        pltpu.make_async_copy(mid, dst, sem_out.at[i]) for i, (_, mid, dst) in enumerate(copies)
-    ]
-    for read in reads:
-        read.start()
-    for read, write in zip(reads, writes):
-        read.wait()
-        write.start()
-    for write in writes:
-        write.wait()
+        copies.append(pltpu.make_async_copy(weights.at[spot], out.at[spot], sem.at[i]))
+    for i, ref in enumerate((master_new, one_new, two_new, grad)):
+        copies.append(pltpu.make_async_copy(results.at[i], ref, sem.at[16 + i]))
+    for copy in copies:
+        copy.start()
+    for copy in copies:
+        copy.wait()
 
 
 def fused(partials, master, moment_one, moment_two):
@@ -517,11 +517,12 @@
     half = full // 2
     dims = (2, 2, 2, 2, 16)
     hbm = pl.BlockSpec(memory_space=pl.ANY)
+    vmem = pl.BlockSpec(memory_space=pltpu.VMEM)
     slab = jax.ShapeDtypeStruct(dims + (full,), BF16)
     dma = pltpu.SemaphoreType.DMA
     results, weights = pl.pallas_call(
         functools.partial(kernel, n, half),
-        out_shape=(jax.ShapeDtypeStruct((4,) + master.shape, F32), slab),
+        out_shape=(pltpu.VMEM((4,) + master.shape, F32), pltpu.VMEM(dims + (full,), BF16)),
         in_specs=[hbm] * 4,
         out_specs=(hbm, hbm),
         scratch_shapes=[
@@ -537,7 +538,8 @@
             pltpu.VMEM((2, 2, 16, half), BF16),
             pltpu.VMEM((2, 2, 16, half), BF16),
             pltpu.VMEM((2, 2, 16, half), F32),
-            pltpu.VMEM((3, 16, half), F32),
+            pltpu.VMEM((2, 2, 16, half), BF16),
+            pltpu.VMEM((3, 16, half), BF16),
             pltpu.VMEM((3, 2, 8, half), F32),
             pltpu.VMEM((4, 2, 8, half), F32),
             pltpu.VMEM(dims + (half,), BF16),
@@ -562,7 +564,7 @@
             dma((CHUNKS, 2)),
         ],
         compiler_params=pltpu.CompilerParams(
-            collective_id=0, has_side_effects=True, vmem_limit_bytes=56 * 2**20
+            collective_id=0, has_side_effects=True, vmem_limit_bytes=52 * 2**20
         ),
         cost_estimate=pl.CostEstimate(
             flops=60 * rows * full, bytes_accessed=6 * rows * full, transcendentals=0
@@ -571,15 +573,12 @@
     outs = pl.pallas_call(
         hand_over,
         out_shape=(jax.ShapeDtypeStruct(master.shape, F32),) * 4 + (slab,),
-        in_specs=[hbm] * 2,
+        in_specs=[vmem] * 2,
         out_specs=(hbm,) * 5,
         scratch_shapes=[
-            pltpu.VMEM((4,) + master.shape, F32),
-            pltpu.VMEM(dims + (full,), BF16),
-            dma((20,)),
             dma((20,)),
         ],
-        compiler_params=pltpu.CompilerParams(vmem_limit_bytes=56 * 2**20),
+        compiler_params=pltpu.CompilerParams(vmem_limit_bytes=8 * 2**20),
         cost_estimate=pl.CostEstimate(
             flops=0, bytes_accessed=5 * rows * full, transcendentals=0
         ),

time: 121 us -> 105 us (0.87)
  Pallas kernels: 120 us -> 104 us
    pallas_call x1, Pallas kernels: 112 us -> 100 us  [fused(): pl.pallas_call(functools.partial(kernel, n, half), out_shape=(pltpu.VMEM(...]
    pallas_call x1, Pallas kernels: 8.03 us -> 4.08 us  [fused(): pl.pallas_call(hand_over, out_shape=(jax.ShapeDtypeStruct(master.shape, F...]
where the time goes in v4:
time: 105 us
  Pallas kernels  104 us (99%)
    pallas_call x1, Pallas kernels, fused(): pl.pallas_call(functools.partial(kernel, n, half), out_shape=(pltpu.VMEM(...  100 us
    pallas_call x1, Pallas kernels, fused(): pl.pallas_call(hand_over, out_shape=(jax.ShapeDtypeStruct(master.shape, F...  4.08 us

profile of v4, /device:TPU:1, one launch (start us, length us, event | category | flops | bytes accessed | tf_op | source)
XLA Modules:
  0.0 104.9 jit_solution(7376092774286549376)
XLA Ops:
  0.6 100.2 %shard_map.83 = (f32[4,8,16384]{2,1,0:T(8,128)S(1)}, bf16[2,2,2,2,16,16384]{5,4,3,2,1,0:T(8,128)(2,1)S(1)}) custom-call(bf16[2,2,2,2,16,16384]{5,4,3,2,1,0:T(8,128)(2,1)} %bitcast.2, f32[8,16384]{1,0:T(8,128)} %master.1, f32[8,16384]{1,0:T(8,128)} %one.1, f32[8,16384]{1,0:T(8,128)} %two.1), custom_call_target="tpu_custom_call" | custom-call | flops 251658240 | bytes 25165824 | tf_op jit(solution)/shard_map/pallas_call | solution.py:523
  100.8 4.1 %shard_map.84 = (f32[8,16384]{1,0:T(8,128)}, f32[8,16384]{1,0:T(8,128)}, f32[8,16384]{1,0:T(8,128)}, f32[8,16384]{1,0:T(8,128)}, bf16[2,2,2,2,16,16384]{5,4,3,2,1,0:T(8,128)(2,1)}) custom-call(f32[4,8,16384]{2,1,0:T(8,128)S(1)} %get-tuple-element.12.results, bf16[2,2,2,2,16,16384]{5,4,3,2,1,0:T(8,128)(2,1)S(1)} %get-tuple-element.13.weights), custom_call_target="tpu_custom_call" | custom-call | bytes 20971520 | tf_op jit(solution)/shard_map/pallas_call | solution.py:573

commit v5 on v4

--- a/solution.py
+++ b/solution.py
@@ -12,6 +12,7 @@
 STEP = 20
 WIDTHS = (8, 8, 12, 12, 8, 8, 4, 4)
 CHUNKS = len(WIDTHS)
+LINE_LAST = (1, 4)
 SWAPS = 4
 F32 = jnp.float32
 BF16 = jnp.bfloat16
@@ -405,7 +406,10 @@
         c = cols(j)
         c_out = cols_out(j)
         spot = (z1, z0, y, x, every, c)
-        start(j, "g1", [gather(j, i, spot, device) for i, device in enumerate(line)])
+        if j in LINE_LAST:
+            start_plane(j, "g1", z1, z0)
+        else:
+            start_line(j, "g1", spot)
         start(
             j,
             "state",
@@ -427,29 +431,44 @@
         kept.append(pltpu.make_async_copy(src, dst, sem))
         kept[-1].start()
 
-    def gather_first(j):
-        arrived(j, "g1")
+    def start_line(j, key, spot):
+        start(j, key, [gather(j, i, spot, device) for i, device in enumerate(line)])
+
+    def start_plane(j, key, a, b):
         ca, cb = streams(j)
         start(
             j,
-            "g2",
+            key,
             [
-                gather(j, 3, (every, every, y, x, every, ca), over_y),
-                gather(j, 4, (every, every, y, x, every, cb), over_x),
+                gather(j, 3, (a, b, y, x, every, ca), over_y),
+                gather(j, 4, (a, b, y, x, every, cb), over_x),
             ],
         )
 
-    def gather_second(j):
-        arrived(j, "g2")
+    def finish_plane(j, key, a, b):
         ca, cb = streams(j)
         start(
             j,
-            "g3",
+            key,
             [
-                gather(j, 5, (every, every, every, x, every, ca), over_x),
-                gather(j, 6, (every, every, y, every, every, cb), over_y),
+                gather(j, 5, (a, b, every, x, every, ca), over_x),
+                gather(j, 6, (a, b, y, every, every, cb), over_y),
             ],
         )
+
+    def gather_first(j):
+        arrived(j, "g1")
+        if j in LINE_LAST:
+            finish_plane(j, "g2", z1, z0)
+        else:
+            start_plane(j, "g2", every, every)
+
+    def gather_second(j):
+        arrived(j, "g2")
+        if j in LINE_LAST:
+            start_line(j, "g3", (z1, z0, every, every, every, cols(j)))
+        else:
+            finish_plane(j, "g3", every, every)
 
     def hand_out(j):
         arrived(j, "g3")

time: 105 us -> 112 us (1.067)
  Pallas kernels: 104 us -> 112 us
    pallas_call x1, Pallas kernels: 100 us -> 108 us  [fused(): pl.pallas_call(functools.partial(kernel, n, half), out_shape=(pltpu.VMEM(...]
where the time goes in v5:
time: 112 us
  Pallas kernels  112 us (100%)
    pallas_call x1, Pallas kernels, fused(): pl.pallas_call(functools.partial(kernel, n, half), out_shape=(pltpu.VMEM(...  108 us
    pallas_call x1, Pallas kernels, fused(): pl.pallas_call(hand_over, out_shape=(jax.ShapeDtypeStruct(master.shape, F...  4.08 us

profile of v5, /device:TPU:1, one launch (start us, length us, event | category | flops | bytes accessed | tf_op | source)
XLA Modules:
  0.0 112.3 jit_solution(1668997605890177331)
XLA Ops:
  0.6 107.6 %shard_map.83 = (f32[4,8,16384]{2,1,0:T(8,128)S(1)}, bf16[2,2,2,2,16,16384]{5,4,3,2,1,0:T(8,128)(2,1)S(1)}) custom-call(bf16[2,2,2,2,16,16384]{5,4,3,2,1,0:T(8,128)(2,1)} %bitcast.2, f32[8,16384]{1,0:T(8,128)} %master.1, f32[8,16384]{1,0:T(8,128)} %one.1, f32[8,16384]{1,0:T(8,128)} %two.1), custom_call_target="tpu_custom_call" | custom-call | flops 251658240 | bytes 25165824 | tf_op jit(solution)/shard_map/pallas_call | solution.py:542
  108.2 4.1 %shard_map.84 = (f32[8,16384]{1,0:T(8,128)}, f32[8,16384]{1,0:T(8,128)}, f32[8,16384]{1,0:T(8,128)}, f32[8,16384]{1,0:T(8,128)}, bf16[2,2,2,2,16,16384]{5,4,3,2,1,0:T(8,128)(2,1)}) custom-call(f32[4,8,16384]{2,1,0:T(8,128)S(1)} %get-tuple-element.12.results, bf16[2,2,2,2,16,16384]{5,4,3,2,1,0:T(8,128)(2,1)S(1)} %get-tuple-element.13.weights), custom_call_target="tpu_custom_call" | custom-call | bytes 20971520 | tf_op jit(solution)/shard_map/pallas_call | solution.py:592
